TPU v7x, 128 devices: a whole 4x4x4 slice. The times are simulated.
128 devices in a mesh: row: 16 (over z_hi, y, core), col: 8 (over x, z_lo).
Axes of the slice: x: 4, y: 4, z: 4 (z_hi: 2, z_lo: 2; z = z_hi * 2 + z_lo), core: 2. Of those that a mesh axis runs over, the one named last changes fastest.
Arguments:
- features: bfloat16 [131072, 128], P(('row', 'col')), may hold values from -6 to 6
- block_rows: int32 [16, 8, 704], P('row', 'col'), may hold values from 0 to 63, as said below
- block_cols: int32 [16, 8, 704], P('row', 'col'), may hold values from 0 to 127
- block_vals: bfloat16 [16, 8, 704, 128, 128], P('row', 'col'), may hold values from -0.0546875 to 0.0546875
- tile_counts: int32 [16, 8], P('row', 'col'), may hold values from 88 to 704
- w_first: bfloat16 [128, 128], replicated, may hold values from -0.5 to 0.5
- b_first: float32 [128], replicated, may hold values from -3 to 3
- w_second: bfloat16 [128, 128], replicated, may hold values from -0.5 to 0.5
- b_second: float32 [128], replicated, may hold values from -3 to 3
Outputs:
- node_out: bfloat16 [131072, 128], P(('row', 'col'))
Inputs may be any that keep to these rules, and one draw needn't show every extreme that they name: Within one tile the pairs (block_rows, block_cols) of all 704 slots are distinct.
All inputs are finite; a program needn't handle non-finite values.
Results may differ from a plain program's by a relative error of at most 0.02.
Values may be sent and summed in bfloat16 or wider, within the bound.
A program may use at most 192 MiB of HBM per device.

v0:
```python
import jax
import jax.numpy as jnp
from jax import lax
from jax.sharding import PartitionSpec as P


def accumulate(total, panel, values, rows, cols, live):
    slots = values.shape[0]
    width = min(32, slots)
    panel_blocks = panel.shape[0]
    row_blocks = total.shape[0]

    def visit(group, running):
        start = group * width
        piece = lax.dynamic_slice_in_dim(values, start, width, 0)
        target = lax.dynamic_slice_in_dim(rows, start, width, 0)
        source = lax.dynamic_slice_in_dim(cols, start, width, 0)
        select = (source[:, None] == jnp.arange(panel_blocks, dtype=jnp.int32)[None, :]).astype(
            jnp.bfloat16
        )
        picked = jnp.einsum(
            "kg,gbf->kbf", select, panel, preferred_element_type=jnp.float32
        ).astype(jnp.bfloat16)
        product = jnp.einsum("kab,kbf->kaf", piece, picked, preferred_element_type=jnp.float32)
        keep = start + jnp.arange(width, dtype=jnp.int32) < live
        place = (
            (target[:, None] == jnp.arange(row_blocks, dtype=jnp.int32)[None, :]) & keep[:, None]
        ).astype(jnp.bfloat16)
        upper = product.astype(jnp.bfloat16)
        lower = (product - upper.astype(jnp.float32)).astype(jnp.bfloat16)
        running = running + jnp.einsum(
            "kg,kaf->gaf", place, upper, preferred_element_type=jnp.float32
        )
        return running + jnp.einsum("kg,kaf->gaf", place, lower, preferred_element_type=jnp.float32)

    groups = slots // width
    return lax.fori_loop(0, groups, visit, total)


def per_device(
    features, block_rows, block_cols, block_vals, tile_counts, w_first, b_first, w_second, b_second
):
    block_size = block_vals.shape[-1]
    channels = features.shape[1]
    slots = block_vals.shape[2]
    values = block_vals.reshape(slots, block_size, block_size)
    rows = block_rows.reshape(slots)
    cols = block_cols.reshape(slots)
    count = tile_counts.reshape(())
    own_rows = features.shape[0]
    row_blocks = lax.axis_size("col") * own_rows // block_size

    def aggregate(inputs):
        panel = lax.all_gather(inputs, "row", axis=0, tiled=True).reshape(-1, block_size, channels)
        empty = jnp.zeros((row_blocks, block_size, channels), jnp.float32)
        partial_value = accumulate(empty, panel, values, rows, cols, count)
        rounded = partial_value.reshape(-1, channels).astype(jnp.bfloat16)
        summed = lax.psum_scatter(rounded, "col", scatter_dimension=0, tiled=True).astype(
            jnp.float32
        )
        return summed.astype(jnp.bfloat16)

    first_agg = aggregate(features)
    hidden = jax.nn.relu(
        jnp.dot(first_agg, w_first, preferred_element_type=jnp.float32) + b_first
    ).astype(jnp.bfloat16)
    second_agg = aggregate(hidden)
    return (jnp.dot(second_agg, w_second, preferred_element_type=jnp.float32) + b_second).astype(
        jnp.bfloat16
    )


def solution(mesh):
    in_specs = (
        P(("row", "col"), None),
        P("row", "col", None),
        P("row", "col", None),
        P("row", "col", None, None, None),
        P("row", "col"),
        P(),
        P(),
        P(),
        P(),
    )
    out_specs = P(("row", "col"), None)
    return jax.shard_map(
        per_device, mesh=mesh, in_specs=in_specs, out_specs=out_specs, check_vma=False
    )
```

profile of v0, /device:TPU:1, one launch (start us, length us, event | category | flops | bytes accessed | tf_op | source)
XLA Modules:
  0.0 1010.4 jit_solution(9775021355228426724)
XLA Ops:
  8.7 60.9 %all-gather.3.cloned.1.call-done = bf16[16384,128]{1,0:T(8,128)(2,1)} async-done(((bf16[1024,128]{1,0:T(8,128)(2,1)}), bf16[16384,128]{1,0:T(8,128)(2,1)}) %all-gather.3.cloned.1.call-update) | async-done | bytes 4194320 | tf_op jit(solution)/shard_map/all_gather | solution.py:54
  69.6 380.9 %while.28 = (s32[]{:T(128)}, f32[64,128,128]{2,0,1:T(8,128)}, s32[704]{0:T(1024)S(1)}, s32[]{:T(128)}, bf16[704,128,128]{2,1,0:T(8,128)(2,1)}, /*index=5*/s32[70...) while((s32[]{:T(128)}, f32[64,128,128]{2,0,1:T(8,128)}, ...), condition=%wide.region_1.0_spmd.clone, body=%wide.region_0.0_spmd.clone.sunk | while | flops 407908416 | bytes 28312728 | solution.py:37
  456.6 48.7 %reduce-scatter.3.cloned.1.call-done = bf16[1024,128]{1,0:T(8,128)(2,1)} async-done(((bf16[8192,128]{1,0:T(8,128)(2,1)}), bf16[1024,128]{1,0:T(8,128)(2,1)}) %reduce-scatter.3.cloned.1.call-update) | async-done | bytes 262160 | tf_op jit(solution)/shard_map/reduce_scatter | solution.py:58
  507.4 58.8 %all-gather.5.cloned.1.call-done = bf16[16384,128]{1,0:T(8,128)(2,1)} async-done(((bf16[1024,128]{1,0:T(8,128)(2,1)}), bf16[16384,128]{1,0:T(8,128)(2,1)}) %all-gather.5.cloned.1.call-update) | async-done | bytes 4194320 | tf_op jit(solution)/shard_map/all_gather | solution.py:54
  566.2 380.9 %while.29 = (s32[]{:T(128)}, f32[64,128,128]{2,0,1:T(8,128)}, s32[704]{0:T(1024)S(1)}, s32[]{:T(128)}, bf16[704,128,128]{2,1,0:T(8,128)(2,1)}, /*index=5*/s32[70...) while((s32[]{:T(128)}, f32[64,128,128]{2,0,1:T(8,128)}, ...), condition=%wide.region_4.5_spmd.clone, body=%wide.region_3.4_spmd.clone.sunk | while | flops 407908416 | bytes 28312728 | solution.py:37
  592.8 6.9 fusion.82
  610.1 6.9 fusion.82
  627.5 6.9 fusion.82
  644.9 6.9 fusion.82
  662.2 6.9 fusion.82
  679.6 6.9 fusion.82
  697.0 6.9 fusion.82
  714.4 6.9 fusion.82
  731.7 6.9 fusion.82
  749.1 6.9 fusion.82
  766.5 6.9 fusion.82
  783.9 6.9 fusion.82
  801.2 6.9 fusion.82
  818.6 6.9 fusion.82
  836.0 6.9 fusion.82
  853.3 6.9 fusion.82
  870.7 6.9 fusion.82
  888.1 6.9 fusion.82
  953.1 48.9 %reduce-scatter.5.cloned.1.call-done = bf16[1024,128]{1,0:T(8,128)(2,1)} async-done(((bf16[8192,128]{1,0:T(8,128)(2,1)}), bf16[1024,128]{1,0:T(8,128)(2,1)}) %reduce-scatter.5.cloned.1.call-update) | async-done | bytes 262160 | tf_op jit(solution)/shard_map/reduce_scatter | solution.py:58
  (314 shorter events, 655.1 us)
Async XLA Ops:
  6.5 498.7 %copy-start = (bf16[128,128]{1,0:T(8,128)(2,1)S(1)}, bf16[128,128]{1,0:T(8,128)(2,1)}, u32[]{:S(2)}) copy-start(bf16[128,128]{1,0:T(8,128)(2,1)} %param.18) | copy-start | bytes 98308
  6.5 63.0 %all-gather.3.cloned.1.call-start = ((), (), s32[]{:S(2)}) async-start(), calls=%async_computation.2 | async-start | bytes 4456448 | tf_op jit(solution)/shard_map/all_gather | solution.py:54
  7.3 498.0 %reduce-scatter.3.cloned.1.call-start = ((), (), s32[]{:S(2)}) async-start(), calls=%async_computation.3 | async-start | bytes 2359296 | tf_op jit(solution)/shard_map/reduce_scatter | solution.py:58
  450.5 54.7 %copy-start.2 = (f32[128]{0:T(128)S(1)}, f32[128]{0:T(128)}, u32[]{:S(2)}) copy-start(f32[128]{0:T(128)} %param.19) | copy-start | bytes 1540
  456.5 109.7 %all-gather.5.cloned.1.call-start = ((), (), s32[]{:S(2)}) async-start(), calls=%async_computation.4 | async-start | bytes 4456448 | tf_op jit(solution)/shard_map/all_gather | solution.py:54
  507.1 494.9 %reduce-scatter.5.cloned.1.call-start = ((), (), s32[]{:S(2)}) async-start(), calls=%async_computation.5 | async-start | bytes 2359296 | tf_op jit(solution)/shard_map/reduce_scatter | solution.py:58
  947.1 54.9 %copy-start.1 = (bf16[128,128]{1,0:T(8,128)(2,1)S(1)}, bf16[128,128]{1,0:T(8,128)(2,1)}, u32[]{:S(2)}) copy-start(bf16[128,128]{1,0:T(8,128)(2,1)} %param.20) | copy-start | bytes 98308
  947.1 54.9 %copy-start.3 = (f32[128]{0:T(128)S(1)}, f32[128]{0:T(128)}, u32[]{:S(2)}) copy-start(f32[128]{0:T(128)} %param.21) | copy-start | bytes 1540
Sparse Core Ops, SparseCore 0:
  9.8 59.7 all-gather.2
  456.6 48.5 reduce-scatter.2
  507.7 58.4 all-gather.4
  953.2 48.7 reduce-scatter.4
where the time goes:
time: 1010 us
  matrix products  729 us (72%)
  waiting for transfers between devices  218 us (22%)
  other arithmetic  30 us (3%)
  local copies, waits for them, and re-layouts  18.7 us (2%)
  between operations  13.2 us (1%)
    dot_general x44, matrix products, visit(): jnp.einsum('kg,kaf->gaf', place, lower, preferred_element_type=jnp.float32)  300 us
    dot_general x44, matrix products, visit(): jnp.einsum('kg,gbf->kbf', select, panel, preferred_element_type=jnp.float32)  211 us
    dot_general x44, matrix products, visit(): jnp.einsum('kg,kaf->gaf', place, upper, preferred_element_type=jnp.float32)  126 us
    all_gather x2, waiting for transfers between devices, aggregate(): lax.all_gather(inputs, 'row', axis=0, tiled=True)  120 us
    reduce_scatter x2, waiting for transfers between devices, aggregate(): lax.psum_scatter(rounded, 'col', scatter_dimension=0, tiled=True)  97.6 us
    dot_general x44, matrix products, visit(): jnp.einsum('kab,kbf->kaf', piece, picked, preferred_element_type=jnp.floa...  87.9 us
    lt x44, other arithmetic, visit(): keep = start + jnp.arange(width, dtype=jnp.int32) < live  28.6 us
  transfers between devices with their start and end apart: 4, of which 4 were waited for; matrix products, arithmetic and copies ran while one was open for 0% of the time, Pallas kernels for 0%

commit v1 on v0

v1 whole, which is shorter than its diff:
```python
import functools

import jax
import jax.numpy as jnp
from jax import lax
from jax.experimental import pallas as pl
from jax.experimental.pallas import tpu as pltpu
from jax.sharding import PartitionSpec as P

UNROLL = 64
LOADS = 8
LANES = 128
RING = 4
ROUNDS_FIRST = 2
ROUNDS_MIDDLE = 2
ROUNDS_LAST = 2


def halves(rounds, own_blocks):
    size = own_blocks // 2 // rounds
    return [
        ((i * size, size), (own_blocks // 2 + i * size, size)) for i in range(rounds)
    ]


def kernel(
    feat,
    rows_ref,
    cols_ref,
    vals_hbm,
    count_ref,
    w1,
    b1,
    w2,
    b2,
    out_ref,
    vals,
    sums,
    panel_one,
    panel_two,
    send_buf,
    far_buf,
    near_buf,
    plane_buf,
    pad_rows,
    pad_cols,
    list_v,
    list_s,
    load_sem,
    local_sem,
    send_sem,
    recv_sem,
):
    slots, bs, ch = vals.shape
    panels = (panel_one, panel_two)
    own_blocks = feat.shape[0]
    row_blocks = send_buf.shape[0]
    row = lax.axis_index("row")
    col = lax.axis_index("col")
    zh, y, core = row // 8, (row // 2) % RING, row % 2
    x, zl = col // 2, col % 2

    def row_of(dz, dy, dk):
        return ((zh + dz) % 2) * 8 + ((y + dy + RING) % RING) * 2 + (core + dk) % 2

    def col_of(dx, dl):
        return ((x + dx + RING) % RING) * 2 + (zl + dl) % 2

    yp, ym = (row_of(0, 1, 0), col), (row_of(0, -1, 0), col)
    zp, sib = (row_of(1, 0, 0), col), (row_of(0, 0, 1), col)
    xp, xm, lp = (row, col_of(1, 0)), (row, col_of(-1, 0)), (row, col_of(0, 1))

    loads = []
    share = slots // LOADS
    for i in range(LOADS):
        part = pl.ds(i * share, share)
        loads.append(pltpu.make_async_copy(vals_hbm.at[part], vals.at[part], load_sem.at[i]))
        loads[-1].start()
    own_copy = pltpu.make_async_copy(
        feat, panel_one.at[pl.ds(row * own_blocks, own_blocks)], local_sem.at[0]
    )
    own_copy.start()

    barrier = pltpu.get_barrier_semaphore()
    for peer in (yp, ym, zp, sib, xp, xm, lp):
        pl.semaphore_signal(barrier, inc=1, device_id=peer, device_id_type=pl.DeviceIdType.MESH)
    pl.semaphore_wait(barrier, 7)

    started = []

    def send(src, dst, peer):
        i = len(started)
        copy = pltpu.make_async_remote_copy(
            src_ref=src,
            dst_ref=dst,
            send_sem=send_sem.at[i],
            recv_sem=recv_sem.at[i],
            device_id=peer,
            device_id_type=pl.DeviceIdType.MESH,
        )
        copy.start()
        started.append(copy)
        return copy

    def gather_round(layer, pair, own_src):
        def at(who, piece):
            return panels[layer].at[pl.ds(who * own_blocks + piece[0], piece[1])]

        def forward(who, piece, peer):
            return send(at(who, piece), at(who, piece), peer)

        a, b = pair
        me = row
        up = {p: send(own_src(p), at(me, p), yp) for p in pair}
        down = {p: send(own_src(p), at(me, p), ym) for p in pair}
        over = {p: send(own_src(p), at(me, p), zp) for p in pair}
        shared = [send(own_src(p), at(me, p), sib) for p in pair]
        yield
        below, above, across = row_of(0, -1, 0), row_of(0, 1, 0), row_of(1, 0, 0)
        up[a].wait_recv()
        up_a = forward(below, a, yp)
        down[b].wait_recv()
        down_b = forward(above, b, ym)
        over_up, over_down = {}, {}
        for p in pair:
            over[p].wait_recv()
            over_up[p] = forward(across, p, yp)
            over_down[p] = forward(across, p, ym)
        up[b].wait_recv()
        down[a].wait_recv()
        for who in (below, above, across):
            for p in pair:
                shared.append(forward(who, p, sib))
        yield
        below2, above2 = row_of(1, -1, 0), row_of(1, 1, 0)
        far, far2 = row_of(0, 2, 0), row_of(1, 2, 0)
        over_up[a].wait_recv()
        up_a2 = forward(below2, a, yp)
        over_down[b].wait_recv()
        down_b2 = forward(above2, b, ym)
        up_a.wait_recv()
        shared.append(forward(far, a, sib))
        down_b.wait_recv()
        shared.append(forward(far, b, sib))
        over_up[b].wait_recv()
        over_down[a].wait_recv()
        for who in (below2, above2):
            for p in pair:
                shared.append(forward(who, p, sib))
        yield
        up_a2.wait_recv()
        shared.append(forward(far2, a, sib))
        down_b2.wait_recv()
        shared.append(forward(far2, b, sib))
        yield
        for copy in shared:
            copy.wait_recv()
        yield

    def build_lists():
        tiles = pad_rows.shape[0]
        lane = lax.broadcasted_iota(jnp.int32, (LANES, LANES), 1)
        depth = lax.broadcasted_iota(jnp.int32, (LANES, LANES), 0)
        place = lax.broadcasted_iota(jnp.int32, (1, LANES), 1)
        live_count = count_ref[0, 0]
        for t in range(tiles):
            width = min(LANES, slots - t * LANES)
            if width < LANES:
                pad_rows[t : t + 1, :] = jnp.zeros((1, LANES), jnp.int32)
                pad_cols[t : t + 1, :] = jnp.zeros((1, LANES), jnp.int32)
            pad_rows[t : t + 1, 0:width] = rows_ref[0, :, t * LANES : t * LANES + width]
            pad_cols[t : t + 1, 0:width] = cols_ref[0, :, t * LANES : t * LANES + width]
        key_rows, key_cols, load_cols, group_cols = [], [], [], []

        def upright(v):
            return jnp.sum(jnp.where(lane == depth, v, 0), axis=1, keepdims=True)

        for t in range(tiles):
            index = place + t * LANES
            group = jnp.where(index < live_count, pad_rows[t : t + 1, :], LANES - 1)
            key = group * 1024 + index
            key_rows.append(key)
            key_cols.append(upright(key))
            load_cols.append(upright(index + pad_cols[t : t + 1, :] * 1024 + group * 131072))
            group_cols.append(upright(group))
        ranks = []
        for t in range(tiles):
            below = jnp.zeros((LANES, LANES), jnp.int32)
            for s in range(tiles):
                below = below + (key_rows[s] < key_cols[t]).astype(jnp.int32)
            ranks.append(jnp.sum(below, axis=1, keepdims=True))
        for t in range(tiles):
            found = jnp.zeros((LANES, LANES), jnp.int32)
            for s in range(tiles):
                found = found + jnp.where(ranks[s] == lane + t * LANES, load_cols[s], 0)
            list_v[t : t + 1, :] = jnp.sum(found, axis=0, keepdims=True)
        upto = jnp.zeros((LANES, LANES), jnp.int32)
        for s in range(tiles):
            upto = upto + (group_cols[s] <= lane).astype(jnp.int32)
        list_v[tiles : tiles + 1, :] = jnp.sum(upto, axis=0, keepdims=True)
        for t in range(tiles + 1, list_v.shape[0]):
            list_v[t : t + 1, :] = jnp.zeros((1, LANES), jnp.int32)
        copy = pltpu.make_async_copy(list_v, list_s, local_sem.at[1])
        copy.start()
        copy.wait()

    def multiply(layer):
        halves_per_row = LANES // UNROLL

        def group(g, carry):
            total, last = carry
            for u in range(UNROLL):
                entry = list_s[g // halves_per_row, (g % halves_per_row) * UNROLL + u]
                slot = entry & 1023
                source = (entry >> 10) & 127
                target = entry >> 17
                product = jnp.dot(
                    vals[slot], panels[layer][source], preferred_element_type=jnp.float32
                )
                total = jnp.where(target == last, total, 0.0) + product
                sums[g * UNROLL + u] = total.astype(jnp.bfloat16)
                last = target
            return total, last

        lax.fori_loop(
            0, slots // UNROLL, group, (jnp.zeros((bs, ch), jnp.float32), jnp.int32(-1))
        )

    tiles = pad_rows.shape[0]

    def collect(owner):
        for j in range(own_blocks):
            r = owner * own_blocks + j
            end = list_s[tiles, r]
            start = jnp.where(r > 0, list_s[tiles, jnp.maximum(r - 1, 0)], 0)
            value = sums[jnp.maximum(end - 1, 0)]
            send_buf[r] = jnp.where(end > start, value, jnp.zeros_like(value))

    def wide(v):
        return v.astype(jnp.float32)

    def scatter(layer, pairs, finish, after):
        for dx in (2, 1, -1, 0):
            for dl in (1, 0):
                collect(col_of(dx, dl))

        def part(dx, dl, piece):
            return send_buf.at[pl.ds(col_of(dx, dl) * own_blocks + piece[0], piece[1])]

        half = own_blocks // 2

        def first(i):
            a, b = pairs[i]
            far, near = {}, {}
            for dl in (1, 0):
                far[dl] = (
                    send(part(2, dl, a), far_buf.at[layer, 0, dl, pl.ds(a[0], a[1])], xp),
                    send(part(2, dl, b), far_buf.at[layer, 1, dl, pl.ds(b[0] - half, b[1])], xm),
                )
            for dl in (1, 0):
                near[dl] = [
                    send(part(1, dl, b), near_buf.at[layer, 0, dl, pl.ds(b[0], b[1])], xp),
                    send(part(-1, dl, a), near_buf.at[layer, 1, dl, pl.ds(a[0], a[1])], xm),
                ]
            return far, near

        def second(i, far, near):
            a, b = pairs[i]
            for dl in (1, 0):
                far[dl][0].wait_recv()
                mine = part(1, dl, a)
                mine[...] = (
                    wide(mine[...]) + wide(far_buf[layer, 0, dl, a[0] : a[0] + a[1]])
                ).astype(jnp.bfloat16)
                near[dl].append(
                    send(mine, near_buf.at[layer, 0, dl, pl.ds(a[0], a[1])], xp)
                )
                far[dl][1].wait_recv()
                mine = part(-1, dl, b)
                mine[...] = (
                    wide(mine[...])
                    + wide(far_buf[layer, 1, dl, b[0] - half : b[0] - half + b[1]])
                ).astype(jnp.bfloat16)
                near[dl].append(
                    send(mine, near_buf.at[layer, 1, dl, pl.ds(b[0], b[1])], xm)
                )

        def summed(dl, p):
            return (
                wide(part(0, dl, p)[...])
                + wide(near_buf[layer, 0, dl, p[0] : p[0] + p[1]])
                + wide(near_buf[layer, 1, dl, p[0] : p[0] + p[1]])
            )

        def third(i, near):
            planes = []
            for copy in near[1]:
                copy.wait_recv()
            for p in pairs[i]:
                mine = part(0, 1, p)
                mine[...] = summed(1, p).astype(jnp.bfloat16)
                planes.append(send(mine, plane_buf.at[layer, pl.ds(p[0], p[1])], lp))
            return planes

        def fourth(i, near, planes):
            for copy in near[0]:
                copy.wait_recv()
            for p, copy in zip(pairs[i], planes):
                copy.wait_recv()
                total = summed(0, p) + wide(plane_buf[layer, p[0] : p[0] + p[1]])
                finish(p, total.astype(jnp.bfloat16).reshape(p[1] * bs, ch))

        state = first(0)
        for i in range(len(pairs)):
            far, near = state
            second(i, far, near)
            if i + 1 < len(pairs):
                state = first(i + 1)
            planes = third(i, near)
            fourth(i, near, planes)
            after(i)

    pairs = halves(ROUNDS_FIRST, own_blocks)
    rounds = [
        gather_round(0, pair, lambda p: feat.at[pl.ds(p[0], p[1])]) for pair in pairs
    ]
    for r in rounds:
        next(r)
    build_lists()
    for _ in range(4):
        for r in rounds:
            next(r)
    own_copy.wait()
    for copy in loads:
        copy.wait()
    multiply(0)

    middle = halves(ROUNDS_MIDDLE, own_blocks)
    live = []

    def hidden(p, agg):
        value = jnp.dot(agg, w1[...], preferred_element_type=jnp.float32) + b1[...]
        value = jnp.maximum(value, 0.0).astype(jnp.bfloat16)
        panel_two[pl.ds(row * own_blocks + p[0], p[1])] = value.reshape(p[1], bs, ch)

    def own_hidden(p):
        return panel_two.at[pl.ds(row * own_blocks + p[0], p[1])]

    def step_all():
        for r in live:
            next(r)

    def after(i):
        step_all()
        live.append(gather_round(1, middle[i], own_hidden))
        next(live[-1])

    before = len(started)
    scatter(0, middle, hidden, after)
    stages = {id(r): len(middle) - i for i, r in enumerate(live)}
    while live:
        for r in list(live):
            if stages[id(r)] == 5:
                live.remove(r)
            else:
                next(r)
                stages[id(r)] += 1
    multiply(1)

    for copy in started[before:]:
        copy.wait_send()

    def final(p, agg):
        value = jnp.dot(agg, w2[...], preferred_element_type=jnp.float32) + b2[...]
        out_ref[p[0] : p[0] + p[1]] = value.astype(jnp.bfloat16).reshape(p[1], bs, ch)

    tail = len(started)
    scatter(1, halves(ROUNDS_LAST, own_blocks), final, lambda i: None)
    for copy in started[:before] + started[tail:]:
        copy.wait_send()


def count_copies():
    gather, scatter_ = 30, 14
    return gather * (ROUNDS_FIRST + ROUNDS_MIDDLE) + scatter_ * (ROUNDS_MIDDLE + ROUNDS_LAST)


def per_device(
    features, block_rows, block_cols, block_vals, tile_counts, w_first, b_first, w_second, b_second
):
    slots, bs = block_vals.shape[2], block_vals.shape[3]
    ch = features.shape[1]
    own_blocks = features.shape[0] // bs
    n_row, n_col = lax.axis_size("row"), lax.axis_size("col")
    panel_blocks = n_row * own_blocks
    row_blocks = n_col * own_blocks
    tiles = -(-slots // LANES)
    half = own_blocks // 2
    bf16 = jnp.bfloat16
    copies = count_copies()
    vmem = pl.BlockSpec(memory_space=pltpu.VMEM)
    hbm = pl.BlockSpec(memory_space=pl.ANY)
    out = pl.pallas_call(
        kernel,
        out_shape=jax.ShapeDtypeStruct((own_blocks, bs, ch), bf16),
        in_specs=[hbm, vmem, vmem, hbm, pl.BlockSpec(memory_space=pltpu.SMEM)] + [vmem] * 4,
        out_specs=vmem,
        scratch_shapes=[
            pltpu.VMEM((slots, bs, bs), bf16),
            pltpu.VMEM((slots, bs, ch), bf16),
            pltpu.VMEM((panel_blocks, bs, ch), bf16),
            pltpu.VMEM((panel_blocks, bs, ch), bf16),
            pltpu.VMEM((row_blocks, bs, ch), bf16),
            pltpu.VMEM((2, 2, 2, half, bs, ch), bf16),
            pltpu.VMEM((2, 2, 2, own_blocks, bs, ch), bf16),
            pltpu.VMEM((2, own_blocks, bs, ch), bf16),
            pltpu.VMEM((tiles, LANES), jnp.int32),
            pltpu.VMEM((tiles, LANES), jnp.int32),
            pltpu.VMEM((8, LANES), jnp.int32),
            pltpu.SMEM((8, LANES), jnp.int32),
            pltpu.SemaphoreType.DMA((LOADS,)),
            pltpu.SemaphoreType.DMA((2,)),
            pltpu.SemaphoreType.DMA((copies,)),
            pltpu.SemaphoreType.DMA((copies,)),
        ],
        compiler_params=pltpu.CompilerParams(
            collective_id=0, has_side_effects=True, vmem_limit_bytes=62 * 2**20
        ),
        cost_estimate=pl.CostEstimate(
            flops=4 * slots * bs * bs * ch, bytes_accessed=slots * bs * bs * 2, transcendentals=0
        ),
        name="two_layers",
    )(
        features.reshape(own_blocks, bs, ch),
        block_rows,
        block_cols,
        block_vals.reshape(slots, bs, bs),
        tile_counts,
        w_first,
        b_first.reshape(1, ch),
        w_second,
        b_second.reshape(1, ch),
    )
    return out.reshape(own_blocks * bs, ch)


def solution(mesh):
    in_specs = (
        P(("row", "col"), None),
        P("row", "col", None),
        P("row", "col", None),
        P("row", "col", None, None, None),
        P("row", "col"),
        P(),
        P(),
        P(),
        P(),
    )
    out_specs = P(("row", "col"), None)
    return jax.shard_map(
        per_device, mesh=mesh, in_specs=in_specs, out_specs=out_specs, check_vma=False
    )
```

time: 1010 us -> 117 us (0.12)
  matrix products: 729 us -> 0 us
  waiting for transfers between devices: 218 us -> 0 us
  Pallas kernels: 0 us -> 113 us
  other arithmetic: 30 us -> 0 us
  local copies, waits for them, and re-layouts: 18.7 us -> 1.67 us
  between operations: 13.2 us -> 0.66 us
    dot_general x178 -> x0, matrix products: 729 us -> none  [the longest x44 300 us: visit(): jnp.einsum('kg,kaf->gaf', place, lower, preferred_element_type=jnp.float32)]
    all_gather x2 -> x0, waiting for transfers between devices: 120 us -> none  [aggregate(): lax.all_gather(inputs, 'row', axis=0, tiled=True)]
    pallas_call x0 -> x1, Pallas kernels: none -> 113 us  [per_device(): pl.pallas_call(kernel, out_shape=jax.ShapeDtypeStruct((own_blocks, bs, ch...]
    reduce_scatter x2 -> x0, waiting for transfers between devices: 97.6 us -> none  [aggregate(): lax.psum_scatter(rounded, 'col', scatter_dimension=0, tiled=True)]
    lt x44 -> x0, other arithmetic: 28.6 us -> none  [visit(): keep = start + jnp.arange(width, dtype=jnp.int32) < live]
    while x2 -> x0, local copies, waits for them, and re-layouts: 11.9 us -> none  [accumulate(): return lax.fori_loop(0, groups, visit, total)]
  transfers between devices with their start and end apart: 4 -> 0, of which waited for: 4 -> 0; matrix products, arithmetic and copies ran while one was open for 0% -> 0% of each run, Pallas kernels for 0% -> 0%
where the time goes in v1:
time: 117 us; the launch traced here: 116 us
  Pallas kernels  113 us (97%)
  local copies, waits for them, and re-layouts  1.67 us (1%)
    pallas_call x1, Pallas kernels, per_device(): pl.pallas_call(kernel, out_shape=jax.ShapeDtypeStruct((own_blocks, bs, ch...  113 us

profile of v1, /device:TPU:1, one launch (start us, length us, event | category | flops | bytes accessed | tf_op | source)
XLA Modules:
  0.0 115.6 jit_solution(11167580245901907947)
XLA Ops:
  0.7 113.3 %two_layers.1 = bf16[8,128,128]{2,1,0:T(8,128)(2,1)} custom-call(bf16[8,128,128]{2,1,0:T(8,128)(2,1)} %bitcast.7, s32[1,1,704]{2,1,0:T(1,128)} %rows_ref.1, s32[1,1,704]{2,1,0:T(1,128)} %cols_ref.1, bf16[704,128,128]{2,1,0:T(8,128)(2,1)} %bitcast.5, s32[1,1]{1,0:T(1,128)S(6)} %copy.11.count_ref, bf16[128,128]{1,0:T(8,128)(2,1)} %w1.1, f32[1,128]{1,0:T(1,128)} %bitcast.8, ...), custom_call_target="tpu_custom_call" | custom-call | flops 5905580032 | bytes 23068672 | tf_op jit(solution)/shard_map/two_layers/pallas_call | solution.py:403
  114.0 1.7 %copy.12 = bf16[1024,128]{1,0:T(8,128)(2,1)} copy(bf16[1024,128]{1,0:T(8,128)(2,1)} %bitcast.6) | data formatting | bytes 524288

commit v2 on v1

v2 whole, which is shorter than its diff:
```python
import functools

import jax
import jax.numpy as jnp
from jax import lax
from jax.experimental import pallas as pl
from jax.experimental.pallas import tpu as pltpu
from jax.sharding import PartitionSpec as P

UNROLL = 176
LOADS = 8
LANES = 128
RING = 4
CUTS_FIRST = (4, 4)
CUTS_MIDDLE = (4, 4)
CUTS_LAST = (4, 4)


def pieces_of(cuts):
    return [(sum(cuts[:i]), size) for i, size in enumerate(cuts)]


def kernel(
    feat,
    rows_hbm,
    cols_hbm,
    vals_hbm,
    count_hbm,
    w1_hbm,
    b1_hbm,
    w2_hbm,
    b2_hbm,
    out_hbm,
    rows_ref,
    cols_ref,
    count_ref,
    w1,
    b1,
    w2,
    b2,
    out_ref,
    vals,
    sums,
    panel_one,
    panel_two,
    send_buf,
    land,
    pad_rows,
    pad_cols,
    list_v,
    list_s,
    small_sem,
    load_sem,
    local_sem,
    send_sem,
    recv_sem,
):
    slots, bs, ch = vals.shape
    panels = (panel_one, panel_two)
    own_blocks = feat.shape[0]
    row_blocks = send_buf.shape[0]
    row = lax.axis_index("row")
    col = lax.axis_index("col")
    zh, y, core = row // 8, (row // 2) % RING, row % 2
    x, zl = col // 2, col % 2

    def row_of(dz, dy, dk):
        return ((zh + dz) % 2) * 8 + ((y + dy + RING) % RING) * 2 + (core + dk) % 2

    def col_of(dx, dl):
        return ((x + dx + RING) % RING) * 2 + (zl + dl) % 2

    yp, ym = (row_of(0, 1, 0), col), (row_of(0, -1, 0), col)
    zp, sib = (row_of(1, 0, 0), col), (row_of(0, 0, 1), col)
    xp, xm, lp = (row, col_of(1, 0)), (row, col_of(-1, 0)), (row, col_of(0, 1))
    y2, x2 = (row_of(0, 2, 0), col), (row, col_of(2, 0))

    small = []
    for src, dst in (
        (count_hbm, count_ref),
        (rows_hbm, rows_ref),
        (cols_hbm, cols_ref),
        (w1_hbm, w1),
        (b1_hbm, b1),
        (w2_hbm, w2),
        (b2_hbm, b2),
    ):
        small.append(pltpu.make_async_copy(src, dst, small_sem.at[len(small)]))
        small[-1].start()
    loads = []
    share = slots // LOADS
    for i in range(LOADS):
        part = pl.ds(i * share, share)
        loads.append(pltpu.make_async_copy(vals_hbm.at[part], vals.at[part], load_sem.at[i]))
        loads[-1].start()
    own_copy = pltpu.make_async_copy(
        feat, panel_one.at[pl.ds(row * own_blocks, own_blocks)], local_sem.at[0]
    )
    own_copy.start()

    barrier = pltpu.get_barrier_semaphore()
    for peer in (yp, ym, zp, sib, xp, xm, lp, y2, x2):
        pl.semaphore_signal(barrier, inc=1, device_id=peer, device_id_type=pl.DeviceIdType.MESH)
    pl.semaphore_wait(barrier, 9)

    started = []

    def send(src, dst, peer):
        i = len(started)
        copy = pltpu.make_async_remote_copy(
            src_ref=src,
            dst_ref=dst,
            send_sem=send_sem.at[i],
            recv_sem=recv_sem.at[i],
            device_id=peer,
            device_id_type=pl.DeviceIdType.MESH,
        )
        copy.start()
        started.append(copy)
        return copy

    def gather_round(layer, piece, own_src):
        def at(who):
            return panels[layer].at[pl.ds(who * own_blocks + piece[0], piece[1])]

        def forward(who, peer):
            return send(at(who), at(who), peer)

        me, mine = row, own_src(piece)
        over = send(mine, at(me), zp)
        far = send(mine, at(me), y2)
        up = send(mine, at(me), yp)
        down = send(mine, at(me), ym)
        shared = [send(mine, at(me), sib)]
        yield
        over.wait_recv()
        over_up = forward(row_of(1, 0, 0), yp)
        over_down = forward(row_of(1, 0, 0), ym)
        shared.append(forward(row_of(1, 0, 0), sib))
        far.wait_recv()
        far_over = forward(row_of(0, 2, 0), zp)
        shared.append(forward(row_of(0, 2, 0), sib))
        yield
        up.wait_recv()
        shared.append(forward(row_of(0, -1, 0), sib))
        down.wait_recv()
        shared.append(forward(row_of(0, 1, 0), sib))
        yield
        over_up.wait_recv()
        shared.append(forward(row_of(1, -1, 0), sib))
        over_down.wait_recv()
        shared.append(forward(row_of(1, 1, 0), sib))
        far_over.wait_recv()
        shared.append(forward(row_of(1, 2, 0), sib))
        yield
        for copy in shared:
            copy.wait_recv()
        yield

    def build_lists():
        tiles = pad_rows.shape[0]
        lane = lax.broadcasted_iota(jnp.int32, (LANES, LANES), 1)
        depth = lax.broadcasted_iota(jnp.int32, (LANES, LANES), 0)
        place = lax.broadcasted_iota(jnp.int32, (1, LANES), 1)
        live_count = count_ref[0, 0]
        for t in range(tiles):
            width = min(LANES, slots - t * LANES)
            if width < LANES:
                pad_rows[t : t + 1, :] = jnp.zeros((1, LANES), jnp.int32)
                pad_cols[t : t + 1, :] = jnp.zeros((1, LANES), jnp.int32)
            pad_rows[t : t + 1, 0:width] = rows_ref[0, :, t * LANES : t * LANES + width]
            pad_cols[t : t + 1, 0:width] = cols_ref[0, :, t * LANES : t * LANES + width]
        key_rows, key_cols, load_cols, group_cols = [], [], [], []

        def upright(v):
            return jnp.sum(jnp.where(lane == depth, v, 0), axis=1, keepdims=True)

        for t in range(tiles):
            index = place + t * LANES
            group = jnp.where(index < live_count, pad_rows[t : t + 1, :], LANES - 1)
            key = group * 1024 + index
            key_rows.append(key)
            key_cols.append(upright(key))
            load_cols.append(upright(index + pad_cols[t : t + 1, :] * 1024 + group * 131072))
            group_cols.append(upright(group))
        ranks = []
        for t in range(tiles):
            below = jnp.zeros((LANES, LANES), jnp.int32)
            for s in range(tiles):
                below = below + (key_rows[s] < key_cols[t]).astype(jnp.int32)
            ranks.append(jnp.sum(below, axis=1, keepdims=True))
        for t in range(tiles):
            found = jnp.zeros((LANES, LANES), jnp.int32)
            for s in range(tiles):
                found = found + jnp.where(ranks[s] == lane + t * LANES, load_cols[s], 0)
            list_v[t : t + 1, :] = jnp.sum(found, axis=0, keepdims=True)
        upto = jnp.zeros((LANES, LANES), jnp.int32)
        for s in range(tiles):
            upto = upto + (group_cols[s] <= lane).astype(jnp.int32)
        list_v[tiles : tiles + 1, :] = jnp.sum(upto, axis=0, keepdims=True)
        for t in range(tiles + 1, list_v.shape[0]):
            list_v[t : t + 1, :] = jnp.zeros((1, LANES), jnp.int32)
        copy = pltpu.make_async_copy(list_v, list_s, local_sem.at[1])
        copy.start()
        copy.wait()

    def multiply(layer):
        def group(g, carry):
            total, last = carry
            for u in range(UNROLL):
                place = g * UNROLL + u
                entry = list_s[place // LANES, place % LANES]
                slot = entry & 1023
                source = (entry >> 10) & 127
                target = entry >> 17
                product = jnp.dot(
                    vals[slot], panels[layer][source], preferred_element_type=jnp.float32
                )
                total = jnp.where(target == last, total, 0.0) + product
                sums[g * UNROLL + u] = total.astype(jnp.bfloat16)
                last = target
            return total, last

        lax.fori_loop(
            0, slots // UNROLL, group, (jnp.zeros((bs, ch), jnp.float32), jnp.int32(-1))
        )

    tiles = pad_rows.shape[0]

    def collect(owner, p):
        for j in range(p[0], p[0] + p[1]):
            r = owner * own_blocks + j
            end = list_s[tiles, r]
            start = jnp.where(r > 0, list_s[tiles, jnp.maximum(r - 1, 0)], 0)
            value = sums[jnp.maximum(end - 1, 0)]
            send_buf[r] = jnp.where(end > start, value, jnp.zeros_like(value))

    def wide(v):
        return v.astype(jnp.float32)

    def scatter(layer, pieces, finish, between, after):
        def part(dx, dl, p):
            return send_buf.at[pl.ds(col_of(dx, dl) * own_blocks + p[0], p[1])]

        def landed(which, p):
            return land.at[layer, which, pl.ds(p[0], p[1])]

        def first(p):
            for dx, dl in ((2, 1), (1, 1), (-1, 1), (2, 0), (1, 0), (-1, 0), (0, 1), (0, 0)):
                collect(col_of(dx, dl), p)
            return (
                send(part(2, 1, p), landed(0, p), lp),
                send(part(1, 1, p), landed(1, p), xp),
                send(part(-1, 1, p), landed(2, p), xm),
                send(part(1, 0, p), landed(3, p), xp),
                send(part(-1, 0, p), landed(4, p), xm),
            )

        def second(p, copies):
            copies[0].wait_recv()
            mine = part(2, 0, p)
            mine[...] = (wide(mine[...]) + wide(landed(0, p)[...])).astype(jnp.bfloat16)
            return copies + (send(mine, landed(5, p), x2),)

        def third(p, copies):
            copies[1].wait_recv()
            copies[2].wait_recv()
            mine = part(0, 1, p)
            total = wide(mine[...]) + wide(landed(1, p)[...]) + wide(landed(2, p)[...])
            mine[...] = total.astype(jnp.bfloat16)
            return copies + (send(mine, landed(6, p), lp),)

        def fourth(p, copies):
            for copy in copies[3:]:
                copy.wait_recv()
            total = wide(part(0, 0, p)[...])
            for which in (3, 4, 5, 6):
                total = total + wide(landed(which, p)[...])
            finish(p, total.astype(jnp.bfloat16).reshape(p[1] * bs, ch))

        state = first(pieces[0])
        for i, p in enumerate(pieces):
            copies = second(p, state)
            if i + 1 < len(pieces):
                state = first(pieces[i + 1])
            copies = third(p, copies)
            between()
            fourth(p, copies)
            after(i)

    rounds = [
        gather_round(0, piece, lambda p: feat.at[pl.ds(p[0], p[1])])
        for piece in pieces_of(CUTS_FIRST)
    ]
    for r in rounds:
        next(r)
    for copy in small:
        copy.wait()
    build_lists()
    for _ in range(4):
        for r in rounds:
            next(r)
    own_copy.wait()
    for copy in loads:
        copy.wait()
    multiply(0)

    middle = pieces_of(CUTS_MIDDLE)
    live = []

    def hidden(p, agg):
        value = jnp.dot(agg, w1[...], preferred_element_type=jnp.float32) + b1[...]
        value = jnp.maximum(value, 0.0).astype(jnp.bfloat16)
        panel_two[pl.ds(row * own_blocks + p[0], p[1])] = value.reshape(p[1], bs, ch)

    def own_hidden(p):
        return panel_two.at[pl.ds(row * own_blocks + p[0], p[1])]

    def step_all():
        for r in list(live):
            if next(r, live) is live:
                live.remove(r)

    def after(i):
        live.append(gather_round(1, middle[i], own_hidden))
        next(live[-1])

    before = len(started)
    scatter(0, middle, hidden, step_all, after)
    while live:
        step_all()
    multiply(1)

    for copy in started[before:]:
        copy.wait_send()

    def final(p, agg):
        value = jnp.dot(agg, w2[...], preferred_element_type=jnp.float32) + b2[...]
        out_ref[p[0] : p[0] + p[1]] = value.astype(jnp.bfloat16).reshape(p[1], bs, ch)
        here = pl.ds(p[0], p[1])
        copy = pltpu.make_async_copy(
            out_ref.at[here], out_hbm.at[here], local_sem.at[2 + len(written)]
        )
        copy.start()
        written.append(copy)

    written = []

    tail = len(started)
    scatter(1, pieces_of(CUTS_LAST), final, lambda: None, lambda i: None)
    for copy in written:
        copy.wait()
    for copy in started[:before] + started[tail:]:
        copy.wait_send()


def count_copies():
    gather, scatter = 16, 7
    return gather * len(CUTS_FIRST + CUTS_MIDDLE) + scatter * len(CUTS_MIDDLE + CUTS_LAST)


def per_device(
    features, block_rows, block_cols, block_vals, tile_counts, w_first, b_first, w_second, b_second
):
    slots, bs = block_vals.shape[2], block_vals.shape[3]
    ch = features.shape[1]
    own_blocks = features.shape[0] // bs
    n_row, n_col = lax.axis_size("row"), lax.axis_size("col")
    panel_blocks = n_row * own_blocks
    row_blocks = n_col * own_blocks
    tiles = -(-slots // LANES)
    bf16 = jnp.bfloat16
    copies = count_copies()
    hbm = pl.BlockSpec(memory_space=pl.ANY)
    out = pl.pallas_call(
        kernel,
        out_shape=jax.ShapeDtypeStruct((own_blocks, bs, ch), bf16),
        in_specs=[hbm] * 9,
        out_specs=hbm,
        scratch_shapes=[
            pltpu.VMEM(block_rows.shape, jnp.int32),
            pltpu.VMEM(block_cols.shape, jnp.int32),
            pltpu.SMEM(tile_counts.shape, jnp.int32),
            pltpu.VMEM(w_first.shape, bf16),
            pltpu.VMEM((1, ch), jnp.float32),
            pltpu.VMEM(w_second.shape, bf16),
            pltpu.VMEM((1, ch), jnp.float32),
            pltpu.VMEM((own_blocks, bs, ch), bf16),
            pltpu.VMEM((slots, bs, bs), bf16),
            pltpu.VMEM((slots, bs, ch), bf16),
            pltpu.VMEM((panel_blocks, bs, ch), bf16),
            pltpu.VMEM((panel_blocks, bs, ch), bf16),
            pltpu.VMEM((row_blocks, bs, ch), bf16),
            pltpu.VMEM((2, 7, own_blocks, bs, ch), bf16),
            pltpu.VMEM((tiles, LANES), jnp.int32),
            pltpu.VMEM((tiles, LANES), jnp.int32),
            pltpu.VMEM((8, LANES), jnp.int32),
            pltpu.SMEM((8, LANES), jnp.int32),
            pltpu.SemaphoreType.DMA((7,)),
            pltpu.SemaphoreType.DMA((LOADS,)),
            pltpu.SemaphoreType.DMA((2 + len(CUTS_LAST),)),
            pltpu.SemaphoreType.DMA((copies,)),
            pltpu.SemaphoreType.DMA((copies,)),
        ],
        compiler_params=pltpu.CompilerParams(
            collective_id=0, has_side_effects=True, vmem_limit_bytes=62 * 2**20
        ),
        cost_estimate=pl.CostEstimate(
            flops=4 * slots * bs * bs * ch, bytes_accessed=slots * bs * bs * 2, transcendentals=0
        ),
        name="two_layers",
    )(
        features.reshape(own_blocks, bs, ch),
        block_rows,
        block_cols,
        block_vals.reshape(slots, bs, bs),
        tile_counts,
        w_first,
        b_first.reshape(1, ch),
        w_second,
        b_second.reshape(1, ch),
    )
    return out.reshape(own_blocks * bs, ch)


def solution(mesh):
    in_specs = (
        P(("row", "col"), None),
        P("row", "col", None),
        P("row", "col", None),
        P("row", "col", None, None, None),
        P("row", "col"),
        P(),
        P(),
        P(),
        P(),
    )
    out_specs = P(("row", "col"), None)
    return jax.shard_map(
        per_device, mesh=mesh, in_specs=in_specs, out_specs=out_specs, check_vma=False
    )
```

time: 117 us -> 102 us (0.87); the launches traced: 116 us -> 102 us
  Pallas kernels: 113 us -> 99.7 us
    pallas_call x1, Pallas kernels: 113 us -> 99.7 us  [per_device(): pl.pallas_call(kernel, out_shape=jax.ShapeDtypeStruct((own_blocks, bs, ch...]
where the time goes in v2:
time: 102 us
  Pallas kernels  99.7 us (98%)
  local copies, waits for them, and re-layouts  1.67 us (2%)
    pallas_call x1, Pallas kernels, per_device(): pl.pallas_call(kernel, out_shape=jax.ShapeDtypeStruct((own_blocks, bs, ch...  99.7 us

profile of v2, /device:TPU:1, one launch (start us, length us, event | category | flops | bytes accessed | tf_op | source)
XLA Modules:
  0.0 102.0 jit_solution(3703651305698690297)
XLA Ops:
  0.7 99.7 %two_layers.1 = bf16[8,128,128]{2,1,0:T(8,128)(2,1)} custom-call(bf16[8,128,128]{2,1,0:T(8,128)(2,1)} %bitcast.7, s32[1,1,704]{2,1,0:T(1,128)} %rows_hbm.1, s32[1,1,704]{2,1,0:T(1,128)} %cols_hbm.1, bf16[704,128,128]{2,1,0:T(8,128)(2,1)} %bitcast.5, s32[1,1]{1,0:T(1,128)S(6)} %copy.11.count_hbm, bf16[128,128]{1,0:T(8,128)(2,1)} %w1_hbm.1, f32[1,128]{1,0:T(1,128)} %bitcast.8, ...), custom_call_target="tpu_custom_call" | custom-call | flops 5905580032 | bytes 23068672 | tf_op jit(solution)/shard_map/two_layers/pallas_call | solution.py:375
  100.3 1.7 %copy.12 = bf16[1024,128]{1,0:T(8,128)(2,1)} copy(bf16[1024,128]{1,0:T(8,128)(2,1)} %bitcast.6) | data formatting | bytes 524288

commit v3 on v2

--- a/solution.py
+++ b/solution.py
@@ -11,7 +11,7 @@
 LOADS = 8
 LANES = 128
 RING = 4
-CUTS_FIRST = (4, 4)
+CUTS_FIRST = (6, 2)
 CUTS_MIDDLE = (4, 4)
 CUTS_LAST = (4, 4)
 
@@ -246,15 +246,19 @@
             return land.at[layer, which, pl.ds(p[0], p[1])]
 
         def first(p):
-            for dx, dl in ((2, 1), (1, 1), (-1, 1), (2, 0), (1, 0), (-1, 0), (0, 1), (0, 0)):
+            copies = []
+            for dx, dl, which, peer in (
+                (2, 1, 0, lp),
+                (1, 1, 1, xp),
+                (-1, 1, 2, xm),
+                (1, 0, 3, xp),
+                (-1, 0, 4, xm),
+            ):
                 collect(col_of(dx, dl), p)
-            return (
-                send(part(2, 1, p), landed(0, p), lp),
-                send(part(1, 1, p), landed(1, p), xp),
-                send(part(-1, 1, p), landed(2, p), xm),
-                send(part(1, 0, p), landed(3, p), xp),
-                send(part(-1, 0, p), landed(4, p), xm),
-            )
+                copies.append(send(part(dx, dl, p), landed(which, p), peer))
+            for dx, dl in ((2, 0), (0, 1), (0, 0)):
+                collect(col_of(dx, dl), p)
+            return tuple(copies)
 
         def second(p, copies):
             copies[0].wait_recv()

time: 102 us -> 101 us (level)
  Pallas kernels: 99.7 us -> 98.2 us
    pallas_call x1, Pallas kernels: 99.7 us -> 98.2 us  [per_device(): pl.pallas_call(kernel, out_shape=jax.ShapeDtypeStruct((own_blocks, bs, ch...]
where the time goes in v3:
time: 101 us
  Pallas kernels  98.2 us (97%)
  local copies, waits for them, and re-layouts  1.67 us (2%)
    pallas_call x1, Pallas kernels, per_device(): pl.pallas_call(kernel, out_shape=jax.ShapeDtypeStruct((own_blocks, bs, ch...  98.2 us

profile of v3, /device:TPU:1, one launch (start us, length us, event | category | flops | bytes accessed | tf_op | source)
XLA Modules:
  0.0 100.6 jit_solution(2759297057987747933)
XLA Ops:
  0.7 98.2 %two_layers.1 = bf16[8,128,128]{2,1,0:T(8,128)(2,1)} custom-call(bf16[8,128,128]{2,1,0:T(8,128)(2,1)} %bitcast.7, s32[1,1,704]{2,1,0:T(1,128)} %rows_hbm.1, s32[1,1,704]{2,1,0:T(1,128)} %cols_hbm.1, bf16[704,128,128]{2,1,0:T(8,128)(2,1)} %bitcast.5, s32[1,1]{1,0:T(1,128)S(6)} %copy.11.count_hbm, bf16[128,128]{1,0:T(8,128)(2,1)} %w1_hbm.1, f32[1,128]{1,0:T(1,128)} %bitcast.8, ...), custom_call_target="tpu_custom_call" | custom-call | flops 5905580032 | bytes 23068672 | tf_op jit(solution)/shard_map/two_layers/pallas_call | solution.py:379
  98.9 1.7 %copy.12 = bf16[1024,128]{1,0:T(8,128)(2,1)} copy(bf16[1024,128]{1,0:T(8,128)(2,1)} %bitcast.6) | data formatting | bytes 524288

commit v4 on v3

--- a/solution.py
+++ b/solution.py
@@ -7,7 +7,7 @@
 from jax.experimental.pallas import tpu as pltpu
 from jax.sharding import PartitionSpec as P
 
-UNROLL = 176
+UNROLL = 352
 LOADS = 8
 LANES = 128
 RING = 4
@@ -75,6 +75,9 @@
     xp, xm, lp = (row, col_of(1, 0)), (row, col_of(-1, 0)), (row, col_of(0, 1))
     y2, x2 = (row_of(0, 2, 0), col), (row, col_of(2, 0))
 
+    barrier = pltpu.get_barrier_semaphore()
+    for peer in (yp, ym, zp, sib, xp, xm, lp, y2, x2):
+        pl.semaphore_signal(barrier, inc=1, device_id=peer, device_id_type=pl.DeviceIdType.MESH)
     small = []
     for src, dst in (
         (count_hbm, count_ref),
@@ -98,9 +101,6 @@
     )
     own_copy.start()
 
-    barrier = pltpu.get_barrier_semaphore()
-    for peer in (yp, ym, zp, sib, xp, xm, lp, y2, x2):
-        pl.semaphore_signal(barrier, inc=1, device_id=peer, device_id_type=pl.DeviceIdType.MESH)
     pl.semaphore_wait(barrier, 9)
 
     started = []

time: 101 us -> 100 us (0.990)
  no operation moved by 1% of the time
where the time goes in v4:
time: 100 us; the launch traced here: 99.9 us
  Pallas kernels  97.5 us (98%)
  local copies, waits for them, and re-layouts  1.67 us (2%)
    pallas_call x1, Pallas kernels, per_device(): pl.pallas_call(kernel, out_shape=jax.ShapeDtypeStruct((own_blocks, bs, ch...  97.5 us

profile of v4, /device:TPU:1, one launch (start us, length us, event | category | flops | bytes accessed | tf_op | source)
XLA Modules:
  0.0 99.9 jit_solution(7782099395947089904)
XLA Ops:
  0.7 97.5 %two_layers.1 = bf16[8,128,128]{2,1,0:T(8,128)(2,1)} custom-call(bf16[8,128,128]{2,1,0:T(8,128)(2,1)} %bitcast.7, s32[1,1,704]{2,1,0:T(1,128)} %rows_hbm.1, s32[1,1,704]{2,1,0:T(1,128)} %cols_hbm.1, bf16[704,128,128]{2,1,0:T(8,128)(2,1)} %bitcast.5, s32[1,1]{1,0:T(1,128)S(6)} %copy.11.count_hbm, bf16[128,128]{1,0:T(8,128)(2,1)} %w1_hbm.1, f32[1,128]{1,0:T(1,128)} %bitcast.8, ...), custom_call_target="tpu_custom_call" | custom-call | flops 5905580032 | bytes 23068672 | tf_op jit(solution)/shard_map/two_layers/pallas_call | solution.py:379
  98.2 1.7 %copy.12 = bf16[1024,128]{1,0:T(8,128)(2,1)} copy(bf16[1024,128]{1,0:T(8,128)(2,1)} %bitcast.6) | data formatting | bytes 524288
